TPU v7x, 32 devices: a whole 2x2x4 slice. The times are simulated.
32 devices in a mesh: row: 8 (over y, x, core), col: 4 (over z).
Axes of the slice: x: 2, y: 2, z: 4, core: 2. Of those that a mesh axis runs over, the one named last changes fastest.
Arguments:
- density: bfloat16 [1024, 1024], P('row', 'col'), as said below
- cotangent: bfloat16 [1024, 1024], P('row', 'col'), may hold values from -6 to 6
- block_pattern: int32 [16, 16], P('row', 'col'), may hold values from 0 to 1, as said below
- filter_pattern: int32 [16, 16], P('row', 'col'), may hold values from 0 to 1, as said below
Outputs:
- purified: bfloat16 [1024, 1024], P('row', 'col')
- gradient: bfloat16 [1024, 1024], P('row', 'col')
Inputs may be any that keep to these rules, and one draw needn't show every extreme that they name: density is symmetric. `block_pattern`: symmetric, with ones on the diagonal. `filter_pattern`: symmetric, with ones on the diagonal.
All inputs are finite; a program needn't handle non-finite values.
Results may differ from a plain program's by a relative error of at most 0.0043.
Values may be sent and summed in bfloat16 or wider, within the bound.
No kernel may reach another device: no remote copies, remote signals or barrier semaphores. Data moves between devices by JAX's collectives and lax.ppermute only.
A program may use at most 64 MiB of HBM per device.

v0:
```python
import jax
import jax.numpy as jnp
from jax import lax
from jax.experimental import pallas as pl
from jax.experimental.pallas import tpu as pltpu
from jax.sharding import PartitionSpec as P

IN_HBM = pl.BlockSpec(memory_space=pltpu.HBM)
IN_VMEM = pl.BlockSpec(memory_space=pltpu.VMEM)
SOON = pl.CostEstimate(flops=100_000_000, bytes_accessed=0, transcendentals=0)
LIMIT = pltpu.CompilerParams(vmem_limit_bytes=32 * 1024 * 1024)
EARLY = pl.CostEstimate(flops=6_000_000_000, bytes_accessed=0, transcendentals=0)


def dot(a, b):
    return jnp.dot(a, b, preferred_element_type=jnp.float32)


def mask(density, cotangent, block_pattern, filter_pattern):
    height, width = density.shape
    block_size = height // block_pattern.shape[0]

    def kernel(*refs):
        pattern_refs, dense_refs = refs[:2], refs[2:4]
        pair_ref, kept_ref, pattern_held, dense_held, sems = refs[4:]
        copies = []
        for k in range(2):
            copies.append(pltpu.make_async_copy(pattern_refs[k], pattern_held.at[k], sems.at[k]))
            copies.append(pltpu.make_async_copy(dense_refs[k], dense_held.at[k], sems.at[2 + k]))
        for copy in copies:
            copy.start()
        for copy in copies:
            copy.wait()
        lane = lax.broadcasted_iota(jnp.int32, (block_size, width), 1) // block_size
        for k in range(2):
            for i in range(height // block_size):
                rows = pl.ds(i * block_size, block_size)
                kept = jnp.zeros((block_size, width), jnp.float32)
                for j in range(width // block_size):
                    kept = jnp.where(lane == j, pattern_held[k, i, j].astype(jnp.float32), kept)
                kept_ref[k, rows, :] = kept
                pair_ref[k, rows, :] = (dense_held[k, rows, :].astype(jnp.float32) * kept).astype(pair_ref.dtype)

    inputs = (block_pattern, filter_pattern, density, cotangent)
    return pl.pallas_call(
        kernel,
        out_shape=(
            pltpu.VMEM((2, height, width), density.dtype),
            pltpu.VMEM((2, height, width), jnp.float32),
        ),
        in_specs=[IN_HBM] * 4,
        out_specs=(IN_VMEM, IN_VMEM),
        scratch_shapes=[
            pltpu.SMEM((2,) + block_pattern.shape, jnp.int32),
            pltpu.VMEM((2, height, width), density.dtype),
            pltpu.SemaphoreType.DMA((4,)),
        ],
        compiler_params=LIMIT,
        name="mask",
    )(*(pltpu.with_memory_space_constraint(x, pltpu.HBM) for x in inputs))


def settle(block, hint):
    def kernel(block_ref, out_ref):
        out_ref[...] = block_ref[...]

    return pl.pallas_call(
        kernel,
        out_shape=pltpu.VMEM(block.shape, block.dtype),
        in_specs=[IN_VMEM],
        out_specs=IN_VMEM,
        cost_estimate=hint,
        compiler_params=LIMIT,
        name="settle",
    )(block)


def flips_of(size):
    flips = []
    while 2 ** len(flips) < size:
        flips.insert(0, 2 ** len(flips))
    return flips


def swap(held, axis_name, size, flips):
    return [
        ([at ^ flip for at in ats], lax.ppermute(blocks, axis_name, [(i, i ^ flip) for i in range(size)]))
        for flip in flips
        for ats, blocks in held
    ]


def double(held, axis_name, size, flips):
    for flip in flips:
        ats = [at for entry in held for at in entry[0]]
        blocks = held[0][1] if len(held) == 1 else jnp.concatenate([entry[1] for entry in held])
        held = held + swap([(ats, blocks)], axis_name, size, [flip])
    return held


def forward(held, axis_name, size, flips):
    held = double(held, axis_name, size, flips[:-2])
    far = swap(held, axis_name, size, flips[-2:-1])
    near = swap(held, axis_name, size, flips[-1:])
    return held + far + near + swap(far, axis_name, size, flips[-1:])


def tie(helds):
    arrays = lax.optimization_barrier([[blocks for _, blocks in held] for held in helds])
    return [[(ats, block) for (ats, _), block in zip(held, blocks)] for held, blocks in zip(helds, arrays)]


def exchange(pair, axis_name, size, tied, later=()):
    flips = flips_of(size)
    held = double([([0], pair[None])], axis_name, size, flips[:-2])
    far = swap(held, axis_name, size, flips[-2:-1])
    near = swap(held, axis_name, size, flips[-1:])
    if tied:
        far, near = tie([far, near])
    else:
        near = [(ats, settle(pairs, SOON)) for ats, pairs in near]
    _, later = tie([far, later])
    last = swap(far, axis_name, size, flips[-1:])
    last = [(ats, settle(pairs, EARLY)) for ats, pairs in last]
    held = held + far + near + last
    return [(at, ((pairs, (k, 0)), (pairs, (k, 1)))) for ats, pairs in held for k, at in enumerate(ats)], later


def part(ref, owner, size):
    return ref.at[pl.ds(pl.multiple_of(owner * size, size), size), :]


def settle(block, hint):
    def kernel(block_ref, out_ref):
        out_ref[...] = block_ref[...]

    return pl.pallas_call(
        kernel,
        out_shape=pltpu.VMEM(block.shape, block.dtype),
        in_specs=[IN_VMEM],
        out_specs=IN_VMEM,
        cost_estimate=hint,
        compiler_params=LIMIT,
        name="settle",
    )(block)


def call(kernel, name, fixed, blocks, pairs, out_shape, scratch=(), hint=None):
    arrays, places = [*fixed], {}
    for array, _ in [block for _, block in blocks] + [block for _, two in pairs for block in two]:
        if id(array) not in places:
            places[id(array)] = len(arrays)
            arrays.append(array)

    def body(*refs):
        def ref_of(block):
            return refs[places[id(block[0])]].at[block[1]]

        here = (lax.axis_index("row"), lax.axis_index("col"))
        block_refs = [(at, ref_of(block)) for at, block in blocks]
        pair_refs = [(at, [ref_of(block) for block in two]) for at, two in pairs]
        kernel(here, refs[:len(fixed)], block_refs, pair_refs, refs[len(arrays):])

    return pl.pallas_call(
        body,
        out_shape=out_shape,
        in_specs=[IN_VMEM] * len(arrays),
        out_specs=jax.tree.map(lambda _: IN_VMEM, out_shape),
        scratch_shapes=scratch,
        cost_estimate=hint,
        compiler_params=LIMIT,
        name=name,
    )(*arrays)


def fill_rows(rows_ref, pieces, here_col):
    height, width = rows_ref.shape[0] // 2, rows_ref.shape[1] // len(pieces)
    for at, blocks in pieces:
        columns = pl.ds(pl.multiple_of((here_col ^ at) * width, width), width)
        for k in range(2):
            rows_ref[k * height:(k + 1) * height, columns] = blocks[k][...]


def square_step(pair, kept, masked_blocks, pair_held):
    _, height, width = pair.shape
    n_row = len(masked_blocks)

    def kernel(here, fixed, blocks, pairs, outs):
        pair_ref, kept_ref = fixed
        both_ref, masked_ref, rows_ref = outs
        fill_rows(rows_ref, pairs, here[1])
        for at, block in blocks:
            part(masked_ref, here[0] ^ at, height)[...] = block[...]
        total = dot(rows_ref[...], masked_ref[...])
        both_ref[0] = (total[:height] * kept_ref[1]).astype(both_ref.dtype)
        grad = 3.0 * pair_ref[1].astype(jnp.float32) - 2.0 * total[height:]
        both_ref[1] = (grad * kept_ref[1]).astype(both_ref.dtype)

    out = (
        pltpu.VMEM((2, height, width), pair.dtype),
        pltpu.VMEM((n_row * height, width), pair.dtype),
        pltpu.VMEM((2 * height, len(pair_held) * width), pair.dtype),
    )
    return call(kernel, "square_step", (pair, kept), masked_blocks, pair_held, out)


def last_step(both, kept, masked_cols, pair_rows, both_held, grad_blocks, filtered_blocks):
    _, height, width = both.shape
    n_row = len(grad_blocks)

    def kernel(here, fixed, blocks, pairs, outs):
        both_ref, kept_ref, masked_ref, pair_ref = fixed
        purified_ref, gradient_ref, rows_ref, late_cols = outs
        fill_rows(rows_ref, pairs, here[1])
        for i, (at, block) in enumerate(blocks):
            part(late_cols.at[i // n_row], here[0] ^ at, height)[...] = block[...]
        total = dot(rows_ref[...], masked_ref[...])
        cubic = total[:height] * kept_ref[1]
        purified_ref[...] = (3.0 * both_ref[0].astype(jnp.float32) - 2.0 * cubic).astype(purified_ref.dtype)
        summed = total[height:] + dot(pair_ref[:height], late_cols[0])
        summed = summed - 2.0 * dot(rows_ref[:height], late_cols[1])
        gradient_ref[...] = (summed * kept_ref[0]).astype(gradient_ref.dtype)

    out = jax.ShapeDtypeStruct((height, width), both.dtype)
    scratch = [
        pltpu.VMEM((2 * height, len(both_held) * width), both.dtype),
        pltpu.VMEM((2, n_row * height, width), both.dtype),
    ]
    fixed = (both, kept, masked_cols, pair_rows)
    return call(kernel, "last_step", fixed, grad_blocks + filtered_blocks, both_held, (out, out), scratch)


def take(held, *inner):
    return [(at, (array, (k,) + inner)) for ats, array in held for k, at in enumerate(ats)]


def cut(held, k):
    return [(ats, array[:, k]) for ats, array in held]


def pairs_of(one, two):
    return [(ats, jnp.stack([first, second], 1)) for (ats, first), (_, second) in zip(one, two)]


def across_cores(lists, n_row):
    ats = [[at for ats, _ in held for at in ats] for held in lists]
    assert all(sorted(a) == sorted(ats[0]) for a in ats)
    flips = flips_of(n_row)[-1:]
    sent = jnp.stack([jnp.concatenate([array for _, array in held]) for held in lists])
    got = [lax.ppermute(sent, "row", [(i, i ^ flip) for i in range(n_row)]) for flip in flips]
    return [
        take(held) + [(at ^ flip, (array, (k, i))) for flip, array in zip(flips, got) for i, at in enumerate(own)]
        for k, (held, own) in enumerate(zip(lists, ats))
    ]


def on_device(n_row, n_col, density, cotangent, block_pattern, filter_pattern):
    chip_flips = flips_of(n_row)[:-1]
    lead, first, second = chip_flips[:-2], chip_flips[-2:-1], chip_flips[-1:]
    pair, kept = mask(density, cotangent, block_pattern, filter_pattern)

    own = double([([0], pair[None])], "row", n_row, lead)
    masked, filtered = cut(own, 0), cut(own, 1)
    pair_held, later = exchange(pair, "col", n_col, False, filtered)
    far = swap(masked, "row", n_row, first)
    near = swap(masked, "row", n_row, second)
    masked = masked + far + near + swap(far, "row", n_row, second)
    other = swap(later, "row", n_row, second)
    (masked_blocks,) = across_cores([masked], n_row)
    both, masked_cols, pair_rows = square_step(pair, kept, masked_blocks, pair_held)

    both_held, _ = exchange(both, "col", n_col, True)
    grad = double([([0], both[1:])], "row", n_row, lead)
    far = swap(grad, "row", n_row, second)
    left = swap(pairs_of(grad, filtered), "row", n_row, first)
    right = swap(pairs_of(far, other), "row", n_row, first)
    grad = grad + far + cut(left, 0) + cut(right, 0)
    filtered = filtered + other + cut(left, 1) + cut(right, 1)
    grad_blocks, filtered_blocks = across_cores([grad, filtered], n_row)
    return last_step(both, kept, masked_cols, pair_rows, both_held, grad_blocks, filtered_blocks)


def solution(mesh):
    placed = (P("row", "col"), P("row", "col"), P("row", "col"), P("row", "col"))

    def local(*arrays):
        return on_device(mesh.shape["row"], mesh.shape["col"], *arrays)

    return jax.shard_map(
        local,
        mesh=mesh,
        in_specs=placed,
        out_specs=(P("row", "col"), P("row", "col")),
        check_vma=False,
    )
```

profile of v0, /device:TPU:0, one launch (start us, length us, event | category | flops | bytes accessed | tf_op | source)
XLA Modules:
  0.0 34.8 jit_solution(7592436583895769551)
XLA Ops:
  0.6 0.9 %mask.1 = (bf16[2,128,256]{2,1,0:T(8,128)(2,1)S(1)}, f32[2,128,256]{2,1,0:T(8,128)S(1)}) custom-call(s32[2,4]{1,0:T(2,128)} %refs_0_.1, s32[2,4]{1,0:T(2,128)} %refs_1_.1, bf16[128,256]{1,0:T(8,128)(2,1)} %refs_2_.1, bf16[128,256]{1,0:T(8,128)(2,1)} %refs_3_.1), custom_call_target="tpu_custom_call" | custom-call | tf_op jit(solution)/shard_map/mask/pallas_call | solution.py:45
  1.6 4.1 %collective-permute-start.4 = (bf16[1,2,128,256]{3,2,1,0:T(8,128)(2,1)S(1)}, bf16[1,2,128,256]{3,2,1,0:T(8,128)(2,1)S(1)}, u32[]{:S(2)}, u32[]{:S(2)}) collective-permute-start(bf16[1,2,128,256]{3,2,1,0:T(8,128)(2,1)S(1)} %bitcast.24), channel_id=1, source_target_pairs={{0,2},{1,3},{2,0},{3,1},{4,6},{5,7},{6,4},{7,5},{8,10},{9,11},{10,... | collective-permute-start | bytes 393224 | tf_op jit(solution)/shard_map/ppermute | solution.py:87
  5.7 1.6 %collective-permute-start = (bf16[1,128,256]{2,1,0:T(8,128)(2,1)S(1)}, bf16[1,128,256]{2,1,0:T(8,128)(2,1)S(1)}, u32[]{:S(2)}, u32[]{:S(2)}) collective-permute-start(bf16[1,128,256]{2,1,0:T(8,128)(2,1)S(1)} %get-tuple-element.24.refs_2_), channel_id=1, source_target_pairs={{0,16},{4,20},{8,24},{12,28},{16,0},{20,4},{24,8},{28,12},{1,17},{... | collective-permute-start | bytes 196616 | tf_op jit(solution)/shard_map/ppermute | solution.py:87
  7.3 1.5 %collective-permute-start.1 = (bf16[1,128,256]{2,1,0:T(8,128)(2,1)S(1)}, bf16[1,128,256]{2,1,0:T(8,128)(2,1)S(1)}, u32[]{:S(2)}, u32[]{:S(2)}) collective-permute-start(bf16[1,128,256]{2,1,0:T(8,128)(2,1)S(1)} %get-tuple-element.24.refs_2_), channel_id=1, source_target_pairs={{0,8},{4,12},{8,0},{12,4},{16,24},{20,28},{24,16},{28,20},{1,9},{5... | collective-permute-start | bytes 196616 | tf_op jit(solution)/shard_map/ppermute | solution.py:87
  8.8 1.3 %collective-permute-done.refs_3_ = bf16[1,128,256]{2,1,0:T(8,128)(2,1)S(1)} collective-permute-done((bf16[1,128,256]{2,1,0:T(8,128)(2,1)S(1)}, bf16[1,128,256]{2,1,0:T(8,128)(2,1)S(1)}, u32[]{:S(2)}, u32[]{:S(2)}) %collective-permute-start) | collective-permute-done | bytes 65568 | tf_op jit(solution)/shard_map/ppermute | solution.py:87
  10.0 1.5 %collective-permute-start.2 = (bf16[1,128,256]{2,1,0:T(8,128)(2,1)S(1)}, bf16[1,128,256]{2,1,0:T(8,128)(2,1)S(1)}, u32[]{:S(2)}, u32[]{:S(2)}) collective-permute-start(bf16[1,128,256]{2,1,0:T(8,128)(2,1)S(1)} %collective-permute-done.refs_3_), channel_id=1, source_target_pairs={{0,8},{4,12},{8,0},{12,4},{16,24},{20,28},{24,16},{28,20},{1,9},{5... | collective-permute-start | bytes 196616 | tf_op jit(solution)/shard_map/ppermute | solution.py:87
  11.5 1.6 %collective-permute-start.5 = (bf16[1,2,128,256]{3,2,1,0:T(8,128)(2,1)S(1)}, bf16[1,2,128,256]{3,2,1,0:T(8,128)(2,1)S(1)}, u32[]{:S(2)}, u32[]{:S(2)}) collective-permute-start(bf16[1,2,128,256]{3,2,1,0:T(8,128)(2,1)S(1)} %bitcast.26), channel_id=1, source_target_pairs={{0,1},{1,0},{2,3},{3,2},{4,5},{5,4},{6,7},{7,6},{8,9},{9,8},{10,11... | collective-permute-start | bytes 393224 | tf_op jit(solution)/shard_map/ppermute | solution.py:87
  13.1 0.5 %collective-permute-start.6 = (bf16[1,2,128,256]{3,2,1,0:T(8,128)(2,1)S(1)}, bf16[1,2,128,256]{3,2,1,0:T(8,128)(2,1)S(1)}, u32[]{:S(2)}, u32[]{:S(2)}) collective-permute-start(bf16[1,2,128,256]{3,2,1,0:T(8,128)(2,1)S(1)} %collective-permute-done.4.refs_8_), channel_id=1, source_target_pairs={{0,1},{1,0},{2,3},{3,2},{4,5},{5,4},{6,7},{7,6},{8,9},{9,8},{10,11... | collective-permute-start | bytes 393224 | tf_op jit(solution)/shard_map/ppermute | solution.py:87
  13.6 0.7 %collective-permute-done.2.refs_5_ = bf16[1,128,256]{2,1,0:T(8,128)(2,1)S(1)} collective-permute-done((bf16[1,128,256]{2,1,0:T(8,128)(2,1)S(1)}, bf16[1,128,256]{2,1,0:T(8,128)(2,1)S(1)}, u32[]{:S(2)}, u32[]{:S(2)}) %collective-permute-start.2) | collective-permute-done | bytes 65568 | tf_op jit(solution)/shard_map/ppermute | solution.py:87
  14.4 1.6 %collective-permute-start.9 = (bf16[1,128,256]{2,1,0:T(8,128)(2,1)S(1)}, bf16[1,128,256]{2,1,0:T(8,128)(2,1)S(1)}, u32[]{:S(2)}, u32[]{:S(2)}) collective-permute-start(bf16[1,128,256]{2,1,0:T(8,128)(2,1)S(1)} %get-tuple-element.15.refs_9_), channel_id=1, source_target_pairs={{0,8},{4,12},{8,0},{12,4},{16,24},{20,28},{24,16},{28,20},{1,9},{5... | collective-permute-start | bytes 196616 | tf_op jit(solution)/shard_map/ppermute | solution.py:87
  16.0 0.7 %collective-permute-done.5.block_ref = bf16[1,2,128,256]{3,2,1,0:T(8,128)(2,1)S(1)} collective-permute-done((bf16[1,2,128,256]{3,2,1,0:T(8,128)(2,1)S(1)}, bf16[1,2,128,256]{3,2,1,0:T(8,128)(2,1)S(1)}, u32[]{:S(2)}, u32[]{:S(2)}) %collective-permute-start.5) | collective-permute-done | bytes 131104 | tf_op jit(solution)/shard_map/ppermute | solution.py:87
  16.7 1.4 %collective-permute-done.6.block_ref = bf16[1,2,128,256]{3,2,1,0:T(8,128)(2,1)S(1)} collective-permute-done((bf16[1,2,128,256]{3,2,1,0:T(8,128)(2,1)S(1)}, bf16[1,2,128,256]{3,2,1,0:T(8,128)(2,1)S(1)}, u32[]{:S(2)}, u32[]{:S(2)}) %collective-permute-start.6) | collective-permute-done | bytes 131104 | tf_op jit(solution)/shard_map/ppermute | solution.py:87
  18.1 0.4 %square_step.1 = (bf16[2,128,256]{2,1,0:T(8,128)(2,1)S(1)}, bf16[1024,256]{1,0:T(8,128)(2,1)S(1)}, bf16[256,1024]{1,0:T(8,128)(2,1)S(1)}) custom-call(bf16[2,128,256]{2,1,0:T(8,128)(2,1)S(1)} %get-tuple-element.10.refs_0_, f32[2,128,256]{2,1,0:T(8,128)S(1)} %get-tuple-element.11.refs_1_, bf16[1,128,256]{2,1,0:T(8,128)(2,1)S(1)} %get-tuple-element.24.refs_2_, ...), custom_call_target="tpu_custom_call" | custom-call | tf_op jit(solution)/shard_map/square_step/pallas_call | solution.py:164
  18.5 1.8 %collective-permute-start.12 = (bf16[1,2,128,256]{3,2,1,0:T(8,128)(2,1)S(1)}, bf16[1,2,128,256]{3,2,1,0:T(8,128)(2,1)S(1)}, u32[]{:S(2)}, u32[]{:S(2)}) collective-permute-start(bf16[1,2,128,256]{3,2,1,0:T(8,128)(2,1)S(1)} %bitcast.28), channel_id=1, source_target_pairs={{0,2},{1,3},{2,0},{3,1},{4,6},{5,7},{6,4},{7,5},{8,10},{9,11},{10,... | collective-permute-start | bytes 393224 | tf_op jit(solution)/shard_map/ppermute | solution.py:87
  20.3 1.9 %collective-permute-start.13 = (bf16[1,2,128,256]{3,2,1,0:T(8,128)(2,1)S(1)}, bf16[1,2,128,256]{3,2,1,0:T(8,128)(2,1)S(1)}, u32[]{:S(2)}, u32[]{:S(2)}) collective-permute-start(bf16[1,2,128,256]{3,2,1,0:T(8,128)(2,1)S(1)} %bitcast.29), channel_id=1, source_target_pairs={{0,1},{1,0},{2,3},{3,2},{4,5},{5,4},{6,7},{7,6},{8,9},{9,8},{10,11... | collective-permute-start | bytes 393224 | tf_op jit(solution)/shard_map/ppermute | solution.py:87
  22.2 1.3 %collective-permute-start.7 = (bf16[1,128,256]{2,1,0:T(8,128)(2,1)S(1)}, bf16[1,128,256]{2,1,0:T(8,128)(2,1)S(1)}, u32[]{:S(2)}, u32[]{:S(2)}) collective-permute-start(bf16[1,128,256]{2,1,0:T(8,128)(2,1)S(1)} %get-tuple-element.26.refs_4_), channel_id=1, source_target_pairs={{0,8},{4,12},{8,0},{12,4},{16,24},{20,28},{24,16},{28,20},{1,9},{5... | collective-permute-start | bytes 196616 | tf_op jit(solution)/shard_map/ppermute | solution.py:87
  23.6 1.6 %collective-permute-start.8 = (bf16[1,2,128,256]{3,2,1,0:T(8,128)(2,1)S(1)}, bf16[1,2,128,256]{3,2,1,0:T(8,128)(2,1)S(1)}, u32[]{:S(2)}, u32[]{:S(2)}) collective-permute-start(bf16[1,2,128,256]{3,2,1,0:T(8,128)(2,1)S(1)} %pad_maximum_fusion.1), channel_id=1, source_target_pairs={{0,16},{4,20},{8,24},{12,28},{16,0},{20,4},{24,8},{28,12},{1,17},{... | collective-permute-start | bytes 393224 | tf_op jit(solution)/shard_map/ppermute | solution.py:87
  25.2 1.3 %collective-permute-done.7.refs_5_ = bf16[1,128,256]{2,1,0:T(8,128)(2,1)S(1)} collective-permute-done((bf16[1,128,256]{2,1,0:T(8,128)(2,1)S(1)}, bf16[1,128,256]{2,1,0:T(8,128)(2,1)S(1)}, u32[]{:S(2)}, u32[]{:S(2)}) %collective-permute-start.7) | collective-permute-done | bytes 65568 | tf_op jit(solution)/shard_map/ppermute | solution.py:87
  26.5 1.6 %collective-permute-start.10 = (bf16[1,2,128,256]{3,2,1,0:T(8,128)(2,1)S(1)}, bf16[1,2,128,256]{3,2,1,0:T(8,128)(2,1)S(1)}, u32[]{:S(2)}, u32[]{:S(2)}) collective-permute-start(bf16[1,2,128,256]{3,2,1,0:T(8,128)(2,1)S(1)} %pad_maximum_fusion.2), channel_id=1, source_target_pairs={{0,16},{4,20},{8,24},{12,28},{16,0},{20,4},{24,8},{28,12},{1,17},{... | collective-permute-start | bytes 393224 | tf_op jit(solution)/shard_map/ppermute | solution.py:87
  28.2 1.6 %collective-permute-done.8 = bf16[1,2,128,256]{3,2,1,0:T(8,128)(2,1)S(1)} collective-permute-done((bf16[1,2,128,256]{3,2,1,0:T(8,128)(2,1)S(1)}, bf16[1,2,128,256]{3,2,1,0:T(8,128)(2,1)S(1)}, u32[]{:S(2)}, u32[]{:S(2)}) %collective-permute-start.8) | collective-permute-done | bytes 131104 | tf_op jit(solution)/shard_map/ppermute | solution.py:87
  29.8 1.7 %collective-permute-done.10 = bf16[1,2,128,256]{3,2,1,0:T(8,128)(2,1)S(1)} collective-permute-done((bf16[1,2,128,256]{3,2,1,0:T(8,128)(2,1)S(1)}, bf16[1,2,128,256]{3,2,1,0:T(8,128)(2,1)S(1)}, u32[]{:S(2)}, u32[]{:S(2)}) %collective-permute-start.10) | collective-permute-done | bytes 131104 | tf_op jit(solution)/shard_map/ppermute | solution.py:87
  31.8 1.3 %collective-permute-done.14.block_ref = bf16[1,2,128,256]{3,2,1,0:T(8,128)(2,1)S(1)} collective-permute-done((bf16[1,2,128,256]{3,2,1,0:T(8,128)(2,1)S(1)}, bf16[1,2,128,256]{3,2,1,0:T(8,128)(2,1)S(1)}, u32[]{:S(2)}, u32[]{:S(2)}) %collective-permute-start.14) | collective-permute-done | bytes 131104 | tf_op jit(solution)/shard_map/ppermute | solution.py:87
  33.1 0.6 %collective-permute-done.11.refs_8_ = bf16[2,4,128,256]{3,2,1,0:T(8,128)(2,1)S(1)} collective-permute-done((bf16[2,4,128,256]{3,2,1,0:T(8,128)(2,1)S(1)}, bf16[2,4,128,256]{3,2,1,0:T(8,128)(2,1)S(1)}, u32[]{:S(2)}, u32[]{:S(2)}) %collective-permute-start.11) | collective-permute-done | bytes 524320 | tf_op jit(solution)/shard_map/ppermute | solution.py:250
  33.7 1.2 %last_step.1 = (bf16[128,256]{1,0:T(8,128)(2,1)}, bf16[128,256]{1,0:T(8,128)(2,1)}) custom-call(bf16[2,128,256]{2,1,0:T(8,128)(2,1)S(1)} %get-tuple-element.12.refs_0_, f32[2,128,256]{2,1,0:T(8,128)S(1)} %get-tuple-element.11.refs_1_, bf16[1024,256]{1,0:T(8,128)(2,1)S(1)} %get-tuple-element.13.refs_2_, bf16[256,1024]{1,0:T(8,128)(2,1)S(1)} %get-tuple-element.14.refs_3_, ...), custom_call_target="tpu_custom_call" | custom-call | tf_op jit(solution)/shard_map/last_step/pallas_call | solution.py:164
  (21 shorter events, 0.5 us)
Async XLA Ops:
  1.6 11.5 %collective-permute-start.4 = (bf16[1,2,128,256]{3,2,1,0:T(8,128)(2,1)S(1)}, bf16[1,2,128,256]{3,2,1,0:T(8,128)(2,1)S(1)}, u32[]{:S(2)}, u32[]{:S(2)}) collective-permute-start(bf16[1,2,128,256]{3,2,1,0:T(8,128)(2,1)S(1)} %bitcast.24), channel_id=1, source_target_pairs={{0,2},{1,3},{2,0},{3,1},{4,6},{5,7},{6,4},{7,5},{8,10},{9,11},{10,... | collective-permute-start | bytes 393224 | tf_op jit(solution)/shard_map/ppermute | solution.py:87
  5.7 4.3 %collective-permute-start = (bf16[1,128,256]{2,1,0:T(8,128)(2,1)S(1)}, bf16[1,128,256]{2,1,0:T(8,128)(2,1)S(1)}, u32[]{:S(2)}, u32[]{:S(2)}) collective-permute-start(bf16[1,128,256]{2,1,0:T(8,128)(2,1)S(1)} %get-tuple-element.24.refs_2_), channel_id=1, source_target_pairs={{0,16},{4,20},{8,24},{12,28},{16,0},{20,4},{24,8},{28,12},{1,17},{... | collective-permute-start | bytes 196616 | tf_op jit(solution)/shard_map/ppermute | solution.py:87
  7.3 6.3 %collective-permute-start.1 = (bf16[1,128,256]{2,1,0:T(8,128)(2,1)S(1)}, bf16[1,128,256]{2,1,0:T(8,128)(2,1)S(1)}, u32[]{:S(2)}, u32[]{:S(2)}) collective-permute-start(bf16[1,128,256]{2,1,0:T(8,128)(2,1)S(1)} %get-tuple-element.24.refs_2_), channel_id=1, source_target_pairs={{0,8},{4,12},{8,0},{12,4},{16,24},{20,28},{24,16},{28,20},{1,9},{5... | collective-permute-start | bytes 196616 | tf_op jit(solution)/shard_map/ppermute | solution.py:87
  10.0 4.3 %collective-permute-start.2 = (bf16[1,128,256]{2,1,0:T(8,128)(2,1)S(1)}, bf16[1,128,256]{2,1,0:T(8,128)(2,1)S(1)}, u32[]{:S(2)}, u32[]{:S(2)}) collective-permute-start(bf16[1,128,256]{2,1,0:T(8,128)(2,1)S(1)} %collective-permute-done.refs_3_), channel_id=1, source_target_pairs={{0,8},{4,12},{8,0},{12,4},{16,24},{20,28},{24,16},{28,20},{1,9},{5... | collective-permute-start | bytes 196616 | tf_op jit(solution)/shard_map/ppermute | solution.py:87
  11.5 5.1 %collective-permute-start.5 = (bf16[1,2,128,256]{3,2,1,0:T(8,128)(2,1)S(1)}, bf16[1,2,128,256]{3,2,1,0:T(8,128)(2,1)S(1)}, u32[]{:S(2)}, u32[]{:S(2)}) collective-permute-start(bf16[1,2,128,256]{3,2,1,0:T(8,128)(2,1)S(1)} %bitcast.26), channel_id=1, source_target_pairs={{0,1},{1,0},{2,3},{3,2},{4,5},{5,4},{6,7},{7,6},{8,9},{9,8},{10,11... | collective-permute-start | bytes 393224 | tf_op jit(solution)/shard_map/ppermute | solution.py:87
  13.1 5.0 %collective-permute-start.6 = (bf16[1,2,128,256]{3,2,1,0:T(8,128)(2,1)S(1)}, bf16[1,2,128,256]{3,2,1,0:T(8,128)(2,1)S(1)}, u32[]{:S(2)}, u32[]{:S(2)}) collective-permute-start(bf16[1,2,128,256]{3,2,1,0:T(8,128)(2,1)S(1)} %collective-permute-done.4.refs_8_), channel_id=1, source_target_pairs={{0,1},{1,0},{2,3},{3,2},{4,5},{5,4},{6,7},{7,6},{8,9},{9,8},{10,11... | collective-permute-start | bytes 393224 | tf_op jit(solution)/shard_map/ppermute | solution.py:87
  14.3 3.8 %collective-permute-start.3 = (bf16[1,4,128,256]{3,2,1,0:T(8,128)(2,1)S(1)}, bf16[1,4,128,256]{3,2,1,0:T(8,128)(2,1)S(1)}, u32[]{:S(2)}, u32[]{:S(2)}) collective-permute-start(bf16[1,4,128,256]{3,2,1,0:T(8,128)(2,1)S(1)} %maximum_bitcast_fusion), channel_id=1, source_target_pairs={{0,4},{4,0},{8,12},{12,8},{16,20},{20,16},{24,28},{28,24},{1,5},{5... | collective-permute-start | bytes 786440 | tf_op jit(solution)/shard_map/ppermute | solution.py:250
  14.4 10.7 %collective-permute-start.9 = (bf16[1,128,256]{2,1,0:T(8,128)(2,1)S(1)}, bf16[1,128,256]{2,1,0:T(8,128)(2,1)S(1)}, u32[]{:S(2)}, u32[]{:S(2)}) collective-permute-start(bf16[1,128,256]{2,1,0:T(8,128)(2,1)S(1)} %get-tuple-element.15.refs_9_), channel_id=1, source_target_pairs={{0,8},{4,12},{8,0},{12,4},{16,24},{20,28},{24,16},{28,20},{1,9},{5... | collective-permute-start | bytes 196616 | tf_op jit(solution)/shard_map/ppermute | solution.py:87
  18.5 9.6 %collective-permute-start.12 = (bf16[1,2,128,256]{3,2,1,0:T(8,128)(2,1)S(1)}, bf16[1,2,128,256]{3,2,1,0:T(8,128)(2,1)S(1)}, u32[]{:S(2)}, u32[]{:S(2)}) collective-permute-start(bf16[1,2,128,256]{3,2,1,0:T(8,128)(2,1)S(1)} %bitcast.28), channel_id=1, source_target_pairs={{0,2},{1,3},{2,0},{3,1},{4,6},{5,7},{6,4},{7,5},{8,10},{9,11},{10,... | collective-permute-start | bytes 393224 | tf_op jit(solution)/shard_map/ppermute | solution.py:87
  20.3 7.8 %collective-permute-start.13 = (bf16[1,2,128,256]{3,2,1,0:T(8,128)(2,1)S(1)}, bf16[1,2,128,256]{3,2,1,0:T(8,128)(2,1)S(1)}, u32[]{:S(2)}, u32[]{:S(2)}) collective-permute-start(bf16[1,2,128,256]{3,2,1,0:T(8,128)(2,1)S(1)} %bitcast.29), channel_id=1, source_target_pairs={{0,1},{1,0},{2,3},{3,2},{4,5},{5,4},{6,7},{7,6},{8,9},{9,8},{10,11... | collective-permute-start | bytes 393224 | tf_op jit(solution)/shard_map/ppermute | solution.py:87
  22.2 4.3 %collective-permute-start.7 = (bf16[1,128,256]{2,1,0:T(8,128)(2,1)S(1)}, bf16[1,128,256]{2,1,0:T(8,128)(2,1)S(1)}, u32[]{:S(2)}, u32[]{:S(2)}) collective-permute-start(bf16[1,128,256]{2,1,0:T(8,128)(2,1)S(1)} %get-tuple-element.26.refs_4_), channel_id=1, source_target_pairs={{0,8},{4,12},{8,0},{12,4},{16,24},{20,28},{24,16},{28,20},{1,9},{5... | collective-permute-start | bytes 196616 | tf_op jit(solution)/shard_map/ppermute | solution.py:87
  23.6 6.2 %collective-permute-start.8 = (bf16[1,2,128,256]{3,2,1,0:T(8,128)(2,1)S(1)}, bf16[1,2,128,256]{3,2,1,0:T(8,128)(2,1)S(1)}, u32[]{:S(2)}, u32[]{:S(2)}) collective-permute-start(bf16[1,2,128,256]{3,2,1,0:T(8,128)(2,1)S(1)} %pad_maximum_fusion.1), channel_id=1, source_target_pairs={{0,16},{4,20},{8,24},{12,28},{16,0},{20,4},{24,8},{28,12},{1,17},{... | collective-permute-start | bytes 393224 | tf_op jit(solution)/shard_map/ppermute | solution.py:87
  26.5 5.0 %collective-permute-start.10 = (bf16[1,2,128,256]{3,2,1,0:T(8,128)(2,1)S(1)}, bf16[1,2,128,256]{3,2,1,0:T(8,128)(2,1)S(1)}, u32[]{:S(2)}, u32[]{:S(2)}) collective-permute-start(bf16[1,2,128,256]{3,2,1,0:T(8,128)(2,1)S(1)} %pad_maximum_fusion.2), channel_id=1, source_target_pairs={{0,16},{4,20},{8,24},{12,28},{16,0},{20,4},{24,8},{28,12},{1,17},{... | collective-permute-start | bytes 393224 | tf_op jit(solution)/shard_map/ppermute | solution.py:87
  28.1 5.0 %collective-permute-start.14 = (bf16[1,2,128,256]{3,2,1,0:T(8,128)(2,1)S(1)}, bf16[1,2,128,256]{3,2,1,0:T(8,128)(2,1)S(1)}, u32[]{:S(2)}, u32[]{:S(2)}) collective-permute-start(bf16[1,2,128,256]{3,2,1,0:T(8,128)(2,1)S(1)} %collective-permute-done.12.refs_14_), channel_id=1, source_target_pairs={{0,1},{1,0},{2,3},{3,2},{4,5},{5,4},{6,7},{7,6},{8,9},{9,8},{10,11... | collective-permute-start | bytes 393224 | tf_op jit(solution)/shard_map/ppermute | solution.py:87
  31.7 2.0 %collective-permute-start.11 = (bf16[2,4,128,256]{3,2,1,0:T(8,128)(2,1)S(1)}, bf16[2,4,128,256]{3,2,1,0:T(8,128)(2,1)S(1)}, u32[]{:S(2)}, u32[]{:S(2)}) collective-permute-start(bf16[2,4,128,256]{3,2,1,0:T(8,128)(2,1)S(1)} %pad_maximum_fusion), channel_id=1, source_target_pairs={{0,4},{4,0},{8,12},{12,8},{16,20},{20,16},{24,28},{28,24},{1,5},{5... | collective-permute-start | bytes 1572872 | tf_op jit(solution)/shard_map/ppermute | solution.py:250
where the time goes:
time: 35 us; the launch traced here: 34.8 us
  starting transfers between devices  20.7 us (59%)
  waiting for transfers between devices  10.6 us (30%)
  Pallas kernels  2.53 us (7%)
  between operations  0.74 us (2%)
    ppermute x13, starting transfers between devices, swap(): lax.ppermute(blocks, axis_name, [(i, i ^ flip) for i in range(size)])  20.6 us
    ppermute x13, waiting for transfers between devices, swap(): lax.ppermute(blocks, axis_name, [(i, i ^ flip) for i in range(size)])  10 us
    pallas_call x2, Pallas kernels, call(): pl.pallas_call(body, out_shape=out_shape, in_specs=[IN_VMEM] * len(arrays...  1.56 us
    pallas_call x1, Pallas kernels, mask(): pl.pallas_call(kernel, out_shape=(pltpu.VMEM((2, height, width), density....  0.94 us
  transfers between devices with their start and end apart: 15, of which 9 were waited for; matrix products, arithmetic and copies ran while one was open for 1% of the time, Pallas kernels for 1%

commit v1 on v0

--- a/solution.py
+++ b/solution.py
@@ -266,7 +266,10 @@
     near = swap(masked, "row", n_row, second)
     masked = masked + far + near + swap(far, "row", n_row, second)
     other = swap(later, "row", n_row, second)
-    (masked_blocks,) = across_cores([masked], n_row)
+    (got,) = across_cores([masked + filtered], n_row)
+    half, count = len(got) // 2, len(take(masked))
+    masked_blocks = got[:count] + got[half:half + count]
+    filtered_blocks = got[count:half] + got[half + count:]
     both, masked_cols, pair_rows = square_step(pair, kept, masked_blocks, pair_held)
 
     both_held, _ = exchange(both, "col", n_col, True)
@@ -275,8 +278,11 @@
     left = swap(pairs_of(grad, filtered), "row", n_row, first)
     right = swap(pairs_of(far, other), "row", n_row, first)
     grad = grad + far + cut(left, 0) + cut(right, 0)
-    filtered = filtered + other + cut(left, 1) + cut(right, 1)
-    grad_blocks, filtered_blocks = across_cores([grad, filtered], n_row)
+    filtered = other + cut(left, 1) + cut(right, 1)
+    (got,) = across_cores([grad + filtered], n_row)
+    half, count = len(got) // 2, len(take(grad))
+    grad_blocks = got[:count] + got[half:half + count]
+    filtered_blocks = filtered_blocks + got[count:half] + got[half + count:]
     return last_step(both, kept, masked_cols, pair_rows, both_held, grad_blocks, filtered_blocks)
 
 

time: 35 us -> 36.7 us (1.049)
  waiting for transfers between devices: 10.6 us -> 15.8 us
  starting transfers between devices: 20.7 us -> 17.3 us
    ppermute x13, waiting for transfers between devices: 10 us -> 14.5 us  [swap(): lax.ppermute(blocks, axis_name, [(i, i ^ flip) for i in range(size)])]
    ppermute x13, starting transfers between devices: 20.6 us -> 17.1 us  [swap(): lax.ppermute(blocks, axis_name, [(i, i ^ flip) for i in range(size)])]
    ppermute x2, waiting for transfers between devices: 0.59 us -> 1.32 us  [across_cores(): lax.ppermute(sent, 'row', [(i, i ^ flip) for i in range(n_row)])]
  transfers between devices with their start and end apart: 15 -> 15, of which waited for: 9 -> 7; matrix products, arithmetic and copies ran while one was open for 1% -> 0% of each run, Pallas kernels for 1% -> 1%
where the time goes in v1:
time: 36.7 us; the launch traced here: 36.6 us
  starting transfers between devices  17.3 us (47%)
  waiting for transfers between devices  15.8 us (43%)
  Pallas kernels  2.53 us (7%)
  between operations  0.79 us (2%)
    ppermute x13, starting transfers between devices, swap(): lax.ppermute(blocks, axis_name, [(i, i ^ flip) for i in range(size)])  17.1 us
    ppermute x13, waiting for transfers between devices, swap(): lax.ppermute(blocks, axis_name, [(i, i ^ flip) for i in range(size)])  14.5 us
    pallas_call x2, Pallas kernels, call(): pl.pallas_call(body, out_shape=out_shape, in_specs=[IN_VMEM] * len(arrays...  1.56 us
    ppermute x2, waiting for transfers between devices, across_cores(): lax.ppermute(sent, 'row', [(i, i ^ flip) for i in range(n_row)])  1.32 us
    pallas_call x1, Pallas kernels, mask(): pl.pallas_call(kernel, out_shape=(pltpu.VMEM((2, height, width), density....  0.94 us
  transfers between devices with their start and end apart: 15, of which 7 were waited for; matrix products, arithmetic and copies ran while one was open for 0% of the time, Pallas kernels for 1%

profile of v1, /device:TPU:0, one launch (start us, length us, event | category | flops | bytes accessed | tf_op | source)
XLA Modules:
  0.0 36.6 jit_solution(9152610905542692056)
XLA Ops:
  0.6 0.9 %mask.1 = (bf16[2,128,256]{2,1,0:T(8,128)(2,1)S(1)}, f32[2,128,256]{2,1,0:T(8,128)S(1)}) custom-call(s32[2,4]{1,0:T(2,128)} %refs_0_.1, s32[2,4]{1,0:T(2,128)} %refs_1_.1, bf16[128,256]{1,0:T(8,128)(2,1)} %refs_2_.1, bf16[128,256]{1,0:T(8,128)(2,1)} %refs_3_.1), custom_call_target="tpu_custom_call" | custom-call | tf_op jit(solution)/shard_map/mask/pallas_call | solution.py:45
  1.6 3.0 %collective-permute-start = (bf16[1,128,256]{2,1,0:T(8,128)(2,1)S(1)}, bf16[1,128,256]{2,1,0:T(8,128)(2,1)S(1)}, u32[]{:S(2)}, u32[]{:S(2)}) collective-permute-start(bf16[1,128,256]{2,1,0:T(8,128)(2,1)S(1)} %get-tuple-element.27.refs_2_), channel_id=1, source_target_pairs={{0,16},{4,20},{8,24},{12,28},{16,0},{20,4},{24,8},{28,12},{1,17},{... | collective-permute-start | bytes 196616 | tf_op jit(solution)/shard_map/ppermute | solution.py:87
  4.6 1.5 %collective-permute-start.1 = (bf16[1,128,256]{2,1,0:T(8,128)(2,1)S(1)}, bf16[1,128,256]{2,1,0:T(8,128)(2,1)S(1)}, u32[]{:S(2)}, u32[]{:S(2)}) collective-permute-start(bf16[1,128,256]{2,1,0:T(8,128)(2,1)S(1)} %get-tuple-element.27.refs_2_), channel_id=1, source_target_pairs={{0,8},{4,12},{8,0},{12,4},{16,24},{20,28},{24,16},{28,20},{1,9},{5... | collective-permute-start | bytes 196616 | tf_op jit(solution)/shard_map/ppermute | solution.py:87
  6.1 2.6 %collective-permute-start.4 = (bf16[1,2,128,256]{3,2,1,0:T(8,128)(2,1)S(1)}, bf16[1,2,128,256]{3,2,1,0:T(8,128)(2,1)S(1)}, u32[]{:S(2)}, u32[]{:S(2)}) collective-permute-start(bf16[1,2,128,256]{3,2,1,0:T(8,128)(2,1)S(1)} %bitcast.32), channel_id=1, source_target_pairs={{0,2},{1,3},{2,0},{3,1},{4,6},{5,7},{6,4},{7,5},{8,10},{9,11},{10,... | collective-permute-start | bytes 393224 | tf_op jit(solution)/shard_map/ppermute | solution.py:87
  8.7 1.6 %collective-permute-start.5 = (bf16[1,2,128,256]{3,2,1,0:T(8,128)(2,1)S(1)}, bf16[1,2,128,256]{3,2,1,0:T(8,128)(2,1)S(1)}, u32[]{:S(2)}, u32[]{:S(2)}) collective-permute-start(bf16[1,2,128,256]{3,2,1,0:T(8,128)(2,1)S(1)} %bitcast.33), channel_id=1, source_target_pairs={{0,1},{1,0},{2,3},{3,2},{4,5},{5,4},{6,7},{7,6},{8,9},{9,8},{10,11... | collective-permute-start | bytes 393224 | tf_op jit(solution)/shard_map/ppermute | solution.py:87
  10.3 0.6 %collective-permute-start.2 = (bf16[1,128,256]{2,1,0:T(8,128)(2,1)S(1)}, bf16[1,128,256]{2,1,0:T(8,128)(2,1)S(1)}, u32[]{:S(2)}, u32[]{:S(2)}) collective-permute-start(bf16[1,128,256]{2,1,0:T(8,128)(2,1)S(1)} %collective-permute-done.refs_3_), channel_id=1, source_target_pairs={{0,8},{4,12},{8,0},{12,4},{16,24},{20,28},{24,16},{28,20},{1,9},{5... | collective-permute-start | bytes 196616 | tf_op jit(solution)/shard_map/ppermute | solution.py:87
  10.9 3.6 %collective-permute-done.4.refs_8_ = bf16[1,2,128,256]{3,2,1,0:T(8,128)(2,1)S(1)} collective-permute-done((bf16[1,2,128,256]{3,2,1,0:T(8,128)(2,1)S(1)}, bf16[1,2,128,256]{3,2,1,0:T(8,128)(2,1)S(1)}, u32[]{:S(2)}, u32[]{:S(2)}) %collective-permute-start.4) | collective-permute-done | bytes 131104 | tf_op jit(solution)/shard_map/ppermute | solution.py:87
  14.5 0.6 %collective-permute-start.6 = (bf16[1,2,128,256]{3,2,1,0:T(8,128)(2,1)S(1)}, bf16[1,2,128,256]{3,2,1,0:T(8,128)(2,1)S(1)}, u32[]{:S(2)}, u32[]{:S(2)}) collective-permute-start(bf16[1,2,128,256]{3,2,1,0:T(8,128)(2,1)S(1)} %collective-permute-done.4.refs_8_), channel_id=1, source_target_pairs={{0,1},{1,0},{2,3},{3,2},{4,5},{5,4},{6,7},{7,6},{8,9},{9,8},{10,11... | collective-permute-start | bytes 393224 | tf_op jit(solution)/shard_map/ppermute | solution.py:87
  15.2 0.1 collective-permute-start.3
  15.3 0.6 %collective-permute-start.9 = (bf16[1,128,256]{2,1,0:T(8,128)(2,1)S(1)}, bf16[1,128,256]{2,1,0:T(8,128)(2,1)S(1)}, u32[]{:S(2)}, u32[]{:S(2)}) collective-permute-start(bf16[1,128,256]{2,1,0:T(8,128)(2,1)S(1)} %get-tuple-element.15.refs_9_), channel_id=1, source_target_pairs={{0,8},{4,12},{8,0},{12,4},{16,24},{20,28},{24,16},{28,20},{1,9},{5... | collective-permute-start | bytes 196616 | tf_op jit(solution)/shard_map/ppermute | solution.py:87
  15.9 3.6 %collective-permute-done.6.block_ref = bf16[1,2,128,256]{3,2,1,0:T(8,128)(2,1)S(1)} collective-permute-done((bf16[1,2,128,256]{3,2,1,0:T(8,128)(2,1)S(1)}, bf16[1,2,128,256]{3,2,1,0:T(8,128)(2,1)S(1)}, u32[]{:S(2)}, u32[]{:S(2)}) %collective-permute-start.6) | collective-permute-done | bytes 131104 | tf_op jit(solution)/shard_map/ppermute | solution.py:87
  19.5 0.4 %square_step.1 = (bf16[2,128,256]{2,1,0:T(8,128)(2,1)S(1)}, bf16[1024,256]{1,0:T(8,128)(2,1)S(1)}, bf16[256,1024]{1,0:T(8,128)(2,1)S(1)}) custom-call(bf16[2,128,256]{2,1,0:T(8,128)(2,1)S(1)} %get-tuple-element.10.refs_0_, f32[2,128,256]{2,1,0:T(8,128)S(1)} %get-tuple-element.11.refs_1_, bf16[1,128,256]{2,1,0:T(8,128)(2,1)S(1)} %get-tuple-element.27.refs_2_, ...), custom_call_target="tpu_custom_call" | custom-call | tf_op jit(solution)/shard_map/square_step/pallas_call | solution.py:164
  20.0 2.4 %collective-permute-start.12 = (bf16[1,2,128,256]{3,2,1,0:T(8,128)(2,1)S(1)}, bf16[1,2,128,256]{3,2,1,0:T(8,128)(2,1)S(1)}, u32[]{:S(2)}, u32[]{:S(2)}) collective-permute-start(bf16[1,2,128,256]{3,2,1,0:T(8,128)(2,1)S(1)} %bitcast.37), channel_id=1, source_target_pairs={{0,2},{1,3},{2,0},{3,1},{4,6},{5,7},{6,4},{7,5},{8,10},{9,11},{10,... | collective-permute-start | bytes 393224 | tf_op jit(solution)/shard_map/ppermute | solution.py:87
  22.4 1.7 %collective-permute-start.13 = (bf16[1,2,128,256]{3,2,1,0:T(8,128)(2,1)S(1)}, bf16[1,2,128,256]{3,2,1,0:T(8,128)(2,1)S(1)}, u32[]{:S(2)}, u32[]{:S(2)}) collective-permute-start(bf16[1,2,128,256]{3,2,1,0:T(8,128)(2,1)S(1)} %bitcast.38), channel_id=1, source_target_pairs={{0,1},{1,0},{2,3},{3,2},{4,5},{5,4},{6,7},{7,6},{8,9},{9,8},{10,11... | collective-permute-start | bytes 393224 | tf_op jit(solution)/shard_map/ppermute | solution.py:87
  24.1 0.5 %collective-permute-start.7 = (bf16[1,128,256]{2,1,0:T(8,128)(2,1)S(1)}, bf16[1,128,256]{2,1,0:T(8,128)(2,1)S(1)}, u32[]{:S(2)}, u32[]{:S(2)}) collective-permute-start(bf16[1,128,256]{2,1,0:T(8,128)(2,1)S(1)} %get-tuple-element.24.refs_4_), channel_id=1, source_target_pairs={{0,8},{4,12},{8,0},{12,4},{16,24},{20,28},{24,16},{28,20},{1,9},{5... | collective-permute-start | bytes 196616 | tf_op jit(solution)/shard_map/ppermute | solution.py:87
  24.7 0.6 %collective-permute-start.8 = (bf16[1,2,128,256]{3,2,1,0:T(8,128)(2,1)S(1)}, bf16[1,2,128,256]{3,2,1,0:T(8,128)(2,1)S(1)}, u32[]{:S(2)}, u32[]{:S(2)}) collective-permute-start(bf16[1,2,128,256]{3,2,1,0:T(8,128)(2,1)S(1)} %pad_maximum_fusion), channel_id=1, source_target_pairs={{0,16},{4,20},{8,24},{12,28},{16,0},{20,4},{24,8},{28,12},{1,17},{... | collective-permute-start | bytes 393224 | tf_op jit(solution)/shard_map/ppermute | solution.py:87
  25.3 3.1 %collective-permute-done.7.refs_5_ = bf16[1,128,256]{2,1,0:T(8,128)(2,1)S(1)} collective-permute-done((bf16[1,128,256]{2,1,0:T(8,128)(2,1)S(1)}, bf16[1,128,256]{2,1,0:T(8,128)(2,1)S(1)}, u32[]{:S(2)}, u32[]{:S(2)}) %collective-permute-start.7) | collective-permute-done | bytes 65568 | tf_op jit(solution)/shard_map/ppermute | solution.py:87
  28.4 0.6 %collective-permute-start.10 = (bf16[1,2,128,256]{3,2,1,0:T(8,128)(2,1)S(1)}, bf16[1,2,128,256]{3,2,1,0:T(8,128)(2,1)S(1)}, u32[]{:S(2)}, u32[]{:S(2)}) collective-permute-start(bf16[1,2,128,256]{3,2,1,0:T(8,128)(2,1)S(1)} %pad_maximum_fusion.1), channel_id=1, source_target_pairs={{0,16},{4,20},{8,24},{12,28},{16,0},{20,4},{24,8},{28,12},{1,17},{... | collective-permute-start | bytes 393224 | tf_op jit(solution)/shard_map/ppermute | solution.py:87
  29.0 0.7 %collective-permute-start.14 = (bf16[1,2,128,256]{3,2,1,0:T(8,128)(2,1)S(1)}, bf16[1,2,128,256]{3,2,1,0:T(8,128)(2,1)S(1)}, u32[]{:S(2)}, u32[]{:S(2)}) collective-permute-start(bf16[1,2,128,256]{3,2,1,0:T(8,128)(2,1)S(1)} %collective-permute-done.12.refs_15_), channel_id=1, source_target_pairs={{0,1},{1,0},{2,3},{3,2},{4,5},{5,4},{6,7},{7,6},{8,9},{9,8},{10,11... | collective-permute-start | bytes 393224 | tf_op jit(solution)/shard_map/ppermute | solution.py:87
  29.7 1.3 %collective-permute-done.8 = bf16[1,2,128,256]{3,2,1,0:T(8,128)(2,1)S(1)} collective-permute-done((bf16[1,2,128,256]{3,2,1,0:T(8,128)(2,1)S(1)}, bf16[1,2,128,256]{3,2,1,0:T(8,128)(2,1)S(1)}, u32[]{:S(2)}, u32[]{:S(2)}) %collective-permute-start.8) | collective-permute-done | bytes 131104 | tf_op jit(solution)/shard_map/ppermute | solution.py:87
  31.0 2.4 %collective-permute-done.10 = bf16[1,2,128,256]{3,2,1,0:T(8,128)(2,1)S(1)} collective-permute-done((bf16[1,2,128,256]{3,2,1,0:T(8,128)(2,1)S(1)}, bf16[1,2,128,256]{3,2,1,0:T(8,128)(2,1)S(1)}, u32[]{:S(2)}, u32[]{:S(2)}) %collective-permute-start.10) | collective-permute-done | bytes 131104 | tf_op jit(solution)/shard_map/ppermute | solution.py:87
  33.6 0.5 %collective-permute-done.14.block_ref = bf16[1,2,128,256]{3,2,1,0:T(8,128)(2,1)S(1)} collective-permute-done((bf16[1,2,128,256]{3,2,1,0:T(8,128)(2,1)S(1)}, bf16[1,2,128,256]{3,2,1,0:T(8,128)(2,1)S(1)}, u32[]{:S(2)}, u32[]{:S(2)}) %collective-permute-start.14) | collective-permute-done | bytes 131104 | tf_op jit(solution)/shard_map/ppermute | solution.py:87
  34.1 1.3 %collective-permute-done.11.refs_8_ = bf16[1,7,128,256]{3,2,1,0:T(8,128)(2,1)S(1)} collective-permute-done((bf16[1,7,128,256]{3,2,1,0:T(8,128)(2,1)S(1)}, bf16[1,7,128,256]{3,2,1,0:T(8,128)(2,1)S(1)}, u32[]{:S(2)}, u32[]{:S(2)}) %collective-permute-start.11) | collective-permute-done | bytes 458784 | tf_op jit(solution)/shard_map/ppermute | solution.py:250
  35.4 1.2 %last_step.1 = (bf16[128,256]{1,0:T(8,128)(2,1)}, bf16[128,256]{1,0:T(8,128)(2,1)}) custom-call(bf16[2,128,256]{2,1,0:T(8,128)(2,1)S(1)} %get-tuple-element.12.refs_0_, f32[2,128,256]{2,1,0:T(8,128)S(1)} %get-tuple-element.11.refs_1_, bf16[1024,256]{1,0:T(8,128)(2,1)S(1)} %get-tuple-element.13.refs_2_, bf16[256,1024]{1,0:T(8,128)(2,1)S(1)} %get-tuple-element.14.refs_3_, ...), custom_call_target="tpu_custom_call" | custom-call | tf_op jit(solution)/shard_map/last_step/pallas_call | solution.py:164
  (29 shorter events, 0.3 us)
Async XLA Ops:
  1.6 8.7 %collective-permute-start = (bf16[1,128,256]{2,1,0:T(8,128)(2,1)S(1)}, bf16[1,128,256]{2,1,0:T(8,128)(2,1)S(1)}, u32[]{:S(2)}, u32[]{:S(2)}) collective-permute-start(bf16[1,128,256]{2,1,0:T(8,128)(2,1)S(1)} %get-tuple-element.27.refs_2_), channel_id=1, source_target_pairs={{0,16},{4,20},{8,24},{12,28},{16,0},{20,4},{24,8},{28,12},{1,17},{... | collective-permute-start | bytes 196616 | tf_op jit(solution)/shard_map/ppermute | solution.py:87
  4.6 6.3 %collective-permute-start.1 = (bf16[1,128,256]{2,1,0:T(8,128)(2,1)S(1)}, bf16[1,128,256]{2,1,0:T(8,128)(2,1)S(1)}, u32[]{:S(2)}, u32[]{:S(2)}) collective-permute-start(bf16[1,128,256]{2,1,0:T(8,128)(2,1)S(1)} %get-tuple-element.27.refs_2_), channel_id=1, source_target_pairs={{0,8},{4,12},{8,0},{12,4},{16,24},{20,28},{24,16},{28,20},{1,9},{5... | collective-permute-start | bytes 196616 | tf_op jit(solution)/shard_map/ppermute | solution.py:87
  6.1 8.4 %collective-permute-start.4 = (bf16[1,2,128,256]{3,2,1,0:T(8,128)(2,1)S(1)}, bf16[1,2,128,256]{3,2,1,0:T(8,128)(2,1)S(1)}, u32[]{:S(2)}, u32[]{:S(2)}) collective-permute-start(bf16[1,2,128,256]{3,2,1,0:T(8,128)(2,1)S(1)} %bitcast.32), channel_id=1, source_target_pairs={{0,2},{1,3},{2,0},{3,1},{4,6},{5,7},{6,4},{7,5},{8,10},{9,11},{10,... | collective-permute-start | bytes 393224 | tf_op jit(solution)/shard_map/ppermute | solution.py:87
  8.7 7.2 %collective-permute-start.5 = (bf16[1,2,128,256]{3,2,1,0:T(8,128)(2,1)S(1)}, bf16[1,2,128,256]{3,2,1,0:T(8,128)(2,1)S(1)}, u32[]{:S(2)}, u32[]{:S(2)}) collective-permute-start(bf16[1,2,128,256]{3,2,1,0:T(8,128)(2,1)S(1)} %bitcast.33), channel_id=1, source_target_pairs={{0,1},{1,0},{2,3},{3,2},{4,5},{5,4},{6,7},{7,6},{8,9},{9,8},{10,11... | collective-permute-start | bytes 393224 | tf_op jit(solution)/shard_map/ppermute | solution.py:87
  10.3 4.9 %collective-permute-start.2 = (bf16[1,128,256]{2,1,0:T(8,128)(2,1)S(1)}, bf16[1,128,256]{2,1,0:T(8,128)(2,1)S(1)}, u32[]{:S(2)}, u32[]{:S(2)}) collective-permute-start(bf16[1,128,256]{2,1,0:T(8,128)(2,1)S(1)} %collective-permute-done.refs_3_), channel_id=1, source_target_pairs={{0,8},{4,12},{8,0},{12,4},{16,24},{20,28},{24,16},{28,20},{1,9},{5... | collective-permute-start | bytes 196616 | tf_op jit(solution)/shard_map/ppermute | solution.py:87
  14.5 5.0 %collective-permute-start.6 = (bf16[1,2,128,256]{3,2,1,0:T(8,128)(2,1)S(1)}, bf16[1,2,128,256]{3,2,1,0:T(8,128)(2,1)S(1)}, u32[]{:S(2)}, u32[]{:S(2)}) collective-permute-start(bf16[1,2,128,256]{3,2,1,0:T(8,128)(2,1)S(1)} %collective-permute-done.4.refs_8_), channel_id=1, source_target_pairs={{0,1},{1,0},{2,3},{3,2},{4,5},{5,4},{6,7},{7,6},{8,9},{9,8},{10,11... | collective-permute-start | bytes 393224 | tf_op jit(solution)/shard_map/ppermute | solution.py:87
  15.2 4.3 %collective-permute-start.3 = (bf16[1,5,128,256]{3,2,1,0:T(8,128)(2,1)S(1)}, bf16[1,5,128,256]{3,2,1,0:T(8,128)(2,1)S(1)}, u32[]{:S(2)}, u32[]{:S(2)}) collective-permute-start(bf16[1,5,128,256]{3,2,1,0:T(8,128)(2,1)S(1)} %bitcast.42), channel_id=1, source_target_pairs={{0,4},{4,0},{8,12},{12,8},{16,20},{20,16},{24,28},{28,24},{1,5},{5... | collective-permute-start | bytes 983048 | tf_op jit(solution)/shard_map/ppermute | solution.py:250
  15.3 10.0 %collective-permute-start.9 = (bf16[1,128,256]{2,1,0:T(8,128)(2,1)S(1)}, bf16[1,128,256]{2,1,0:T(8,128)(2,1)S(1)}, u32[]{:S(2)}, u32[]{:S(2)}) collective-permute-start(bf16[1,128,256]{2,1,0:T(8,128)(2,1)S(1)} %get-tuple-element.15.refs_9_), channel_id=1, source_target_pairs={{0,8},{4,12},{8,0},{12,4},{16,24},{20,28},{24,16},{28,20},{1,9},{5... | collective-permute-start | bytes 196616 | tf_op jit(solution)/shard_map/ppermute | solution.py:87
  20.0 9.0 %collective-permute-start.12 = (bf16[1,2,128,256]{3,2,1,0:T(8,128)(2,1)S(1)}, bf16[1,2,128,256]{3,2,1,0:T(8,128)(2,1)S(1)}, u32[]{:S(2)}, u32[]{:S(2)}) collective-permute-start(bf16[1,2,128,256]{3,2,1,0:T(8,128)(2,1)S(1)} %bitcast.37), channel_id=1, source_target_pairs={{0,2},{1,3},{2,0},{3,1},{4,6},{5,7},{6,4},{7,5},{8,10},{9,11},{10,... | collective-permute-start | bytes 393224 | tf_op jit(solution)/shard_map/ppermute | solution.py:87
  22.4 6.6 %collective-permute-start.13 = (bf16[1,2,128,256]{3,2,1,0:T(8,128)(2,1)S(1)}, bf16[1,2,128,256]{3,2,1,0:T(8,128)(2,1)S(1)}, u32[]{:S(2)}, u32[]{:S(2)}) collective-permute-start(bf16[1,2,128,256]{3,2,1,0:T(8,128)(2,1)S(1)} %bitcast.38), channel_id=1, source_target_pairs={{0,1},{1,0},{2,3},{3,2},{4,5},{5,4},{6,7},{7,6},{8,9},{9,8},{10,11... | collective-permute-start | bytes 393224 | tf_op jit(solution)/shard_map/ppermute | solution.py:87
  24.1 4.3 %collective-permute-start.7 = (bf16[1,128,256]{2,1,0:T(8,128)(2,1)S(1)}, bf16[1,128,256]{2,1,0:T(8,128)(2,1)S(1)}, u32[]{:S(2)}, u32[]{:S(2)}) collective-permute-start(bf16[1,128,256]{2,1,0:T(8,128)(2,1)S(1)} %get-tuple-element.24.refs_4_), channel_id=1, source_target_pairs={{0,8},{4,12},{8,0},{12,4},{16,24},{20,28},{24,16},{28,20},{1,9},{5... | collective-permute-start | bytes 196616 | tf_op jit(solution)/shard_map/ppermute | solution.py:87
  24.7 6.3 %collective-permute-start.8 = (bf16[1,2,128,256]{3,2,1,0:T(8,128)(2,1)S(1)}, bf16[1,2,128,256]{3,2,1,0:T(8,128)(2,1)S(1)}, u32[]{:S(2)}, u32[]{:S(2)}) collective-permute-start(bf16[1,2,128,256]{3,2,1,0:T(8,128)(2,1)S(1)} %pad_maximum_fusion), channel_id=1, source_target_pairs={{0,16},{4,20},{8,24},{12,28},{16,0},{20,4},{24,8},{28,12},{1,17},{... | collective-permute-start | bytes 393224 | tf_op jit(solution)/shard_map/ppermute | solution.py:87
  28.4 5.0 %collective-permute-start.10 = (bf16[1,2,128,256]{3,2,1,0:T(8,128)(2,1)S(1)}, bf16[1,2,128,256]{3,2,1,0:T(8,128)(2,1)S(1)}, u32[]{:S(2)}, u32[]{:S(2)}) collective-permute-start(bf16[1,2,128,256]{3,2,1,0:T(8,128)(2,1)S(1)} %pad_maximum_fusion.1), channel_id=1, source_target_pairs={{0,16},{4,20},{8,24},{12,28},{16,0},{20,4},{24,8},{28,12},{1,17},{... | collective-permute-start | bytes 393224 | tf_op jit(solution)/shard_map/ppermute | solution.py:87
  29.0 5.0 %collective-permute-start.14 = (bf16[1,2,128,256]{3,2,1,0:T(8,128)(2,1)S(1)}, bf16[1,2,128,256]{3,2,1,0:T(8,128)(2,1)S(1)}, u32[]{:S(2)}, u32[]{:S(2)}) collective-permute-start(bf16[1,2,128,256]{3,2,1,0:T(8,128)(2,1)S(1)} %collective-permute-done.12.refs_15_), channel_id=1, source_target_pairs={{0,1},{1,0},{2,3},{3,2},{4,5},{5,4},{6,7},{7,6},{8,9},{9,8},{10,11... | collective-permute-start | bytes 393224 | tf_op jit(solution)/shard_map/ppermute | solution.py:87
  33.5 1.9 %collective-permute-start.11 = (bf16[1,7,128,256]{3,2,1,0:T(8,128)(2,1)S(1)}, bf16[1,7,128,256]{3,2,1,0:T(8,128)(2,1)S(1)}, u32[]{:S(2)}, u32[]{:S(2)}) collective-permute-start(bf16[1,7,128,256]{3,2,1,0:T(8,128)(2,1)S(1)} %bitcast.43), channel_id=1, source_target_pairs={{0,4},{4,0},{8,12},{12,8},{16,20},{20,16},{24,28},{28,24},{1,5},{5... | collective-permute-start | bytes 1376264 | tf_op jit(solution)/shard_map/ppermute | solution.py:250
